TPU v7x, 768 devices: a whole 4x8x12 slice. The times are simulated.
768 devices in a mesh: dp: 24 (over y_hi, z), tensor: 32 (over x, y_lo, core).
Axes of the slice: x: 4, y: 8 (y_hi: 2, y_lo: 4; y = y_hi * 4 + y_lo), z: 12, core: 2. Of those that a mesh axis runs over, the one named last changes fastest.
Arguments:
- tokens: bfloat16 [192, 12288], P('tensor', 'dp'), may hold values from -6 to 6
- gate_weight: bfloat16 [12288, 28672], P('dp', 'tensor'), may hold values from -0.0546875 to 0.0546875
- up_weight: bfloat16 [12288, 28672], P('dp', 'tensor'), may hold values from -0.0546875 to 0.0546875
- down_weight: bfloat16 [28672, 12288], P('tensor', 'dp'), may hold values from -0.03125 to 0.03125
- out_grad: bfloat16 [192, 12288], P('tensor', 'dp'), may hold values from -0.29882812 to 0.29882812
Outputs:
- mixed: bfloat16 [192, 12288], P('tensor', 'dp')
- down_grad: bfloat16 [28672, 12288], P('tensor', 'dp')
All inputs are finite; a program needn't handle non-finite values.
Results may differ from a plain program's by a relative error of at most 0.0049.
Values may be sent and summed in bfloat16 or wider, within the bound.
No kernel may reach another device: no remote copies, remote signals or barrier semaphores. Data moves between devices by JAX's collectives and lax.ppermute only.
A program may use at most 32 MiB of HBM per device.

v0:
```python
import jax
import jax.numpy as jnp
from jax import lax
from jax.sharding import PartitionSpec as P


def activate(summed, hidden_width):
    gate_values = summed[:, :hidden_width]
    up_values = summed[:, hidden_width:]
    return (jax.nn.silu(gate_values) * up_values).astype(jnp.bfloat16)


def body(tokens, gate_weight, up_weight, down_weight, out_grad):
    hidden_width = gate_weight.shape[1]
    gathered, cotangent = (
        lax.all_gather(tokens, "tensor", axis=0, tiled=True),
        lax.all_gather(out_grad, "tensor", axis=0, tiled=True),
    )
    paired = jnp.concatenate([gate_weight, up_weight], axis=1)
    segment = gathered
    summed = lax.psum_scatter(
        jnp.dot(segment, paired, preferred_element_type=jnp.float32),
        "dp",
        scatter_dimension=0,
        tiled=True,
    )
    summed_all = lax.all_gather(summed, "dp", axis=0, tiled=True)
    hidden = activate(summed_all, hidden_width)
    segment = hidden
    mixed = lax.psum_scatter(
        jnp.dot(segment, down_weight, preferred_element_type=jnp.float32),
        "tensor",
        scatter_dimension=0,
        tiled=True,
    ).astype(jnp.bfloat16)
    contract = (((0,), (0,)), ((), ()))
    down_grad = lax.dot_general(hidden, cotangent, contract, preferred_element_type=jnp.float32)
    return (mixed, down_grad.astype(jnp.bfloat16))


def solution(mesh):
    placed = (
        P("tensor", "dp"),
        P("dp", "tensor"),
        P("dp", "tensor"),
        P("tensor", "dp"),
        P("tensor", "dp"),
    )
    return jax.shard_map(
        body,
        mesh=mesh,
        in_specs=placed,
        out_specs=(P("tensor", "dp"), P("tensor", "dp")),
        check_vma=False,
    )
```

profile of v0, /device:TPU:1, one launch (start us, length us, event | category | flops | bytes accessed | tf_op | source)
XLA Modules:
  0.0 719.8 jit_solution(5549161978969394186)
XLA Ops:
  7.2 0.0 copy-start
  7.2 0.0 reduce-scatter.4.cloned.1.call-start
  7.2 49.4 %all-gather = bf16[32,6,512]{2,1,0:T(8,128)(2,1)S(1)} all-gather(bf16[1,6,512]{2,1,0:T(8,128)(2,1)} %bitcast.12), channel_id=1, replica_groups=mesh['dp'=24,'tensor'=32] {'tensor'}, dimensions={0}, use_global_device_ids=true | all-gather | bytes 202752 | tf_op jit(solution)/shard_map/all_gather | solution.py:16
  56.6 0.1 reshape.5
  56.7 3.1 convolution_bitcast_fusion
  59.8 0.0 reduce-scatter.4.cloned.1.call-update
  59.8 0.0 all-gather.4.cloned.1.call-start
  59.8 382.2 %reduce-scatter.4.cloned.1.call-done = f32[8,1792]{1,0:T(8,128)} async-done(((f32[192,1792]{1,0:T(8,128)}), f32[8,1792]{1,0:T(8,128)}) %reduce-scatter.4.cloned.1.call-update) | async-done | bytes 57360 | tf_op jit(solution)/shard_map/reduce_scatter | solution.py:21
  442.0 0.0 all-gather.4.cloned.1.call-update
  442.1 127.3 %all-gather.4.cloned.1.call-done = f32[192,1792]{1,0:T(8,128)} async-done(((f32[8,1792]{1,0:T(8,128)}), f32[192,1792]{1,0:T(8,128)}) %all-gather.4.cloned.1.call-update) | async-done | bytes 1376272 | tf_op jit(solution)/shard_map/all_gather | solution.py:27
  569.4 1.5 fusion.4
  570.9 0.0 copy-start.1
  570.9 0.4 fusion.7
  571.3 76.3 %fusion = f32[8,512]{1,0:T(8,128)S(1)} fusion(f32[192,512]{1,0:T(8,128)S(1)} %fusion.7), kind=kCustom, calls=%all-reduce-scatter | all-reduce-scatter fusion | flops 131073 | bytes 413696
  647.6 2.9 collective-permute-start
  650.4 1.3 collective-permute-start.1
  651.8 1.3 collective-permute-start.7
  653.1 43.1 %all-gather.1 = bf16[32,6,512]{2,1,0:T(8,128)(2,1)S(1)} all-gather(bf16[1,6,512]{2,1,0:T(8,128)(2,1)S(1)} %bitcast.13), channel_id=1, replica_groups=mesh['dp'=24,'tensor'=32] {'tensor'}, dimensions={0}, use_global_device_ids=true | all-gather | bytes 202752 | tf_op jit(solution)/shard_map/all_gather | solution.py:17
  696.2 0.1 reshape.7
  696.3 1.3 dynamic-slice.4
  698.2 1.3 collective-permute-start.2
  699.5 1.3 collective-permute-start.3
  700.8 0.0 collective-permute-done.7
  700.8 1.3 collective-permute-start.4
  702.1 0.0 collective-permute-done
  702.1 3.0 collective-permute-start.5
  705.1 4.9 collective-permute-start.6
  710.1 1.4 convolution_convert_fusion
  711.4 0.0 collective-permute-done.4
  711.5 0.0 collective-permute-done.6
  711.5 0.8 concatenate.4
  712.3 0.6 dynamic-slice_convert_fusion
  (8 shorter events, 0.0 us)
Async XLA Ops:
  7.2 563.7 %copy-start = (bf16[896,512]{1,0:T(8,128)(2,1)S(1)}, bf16[896,512]{1,0:T(8,128)(2,1)}, u32[]{:S(2)}) copy-start(bf16[896,512]{1,0:T(8,128)(2,1)} %param.8) | copy-start | bytes 2752516
  7.2 434.8 %reduce-scatter.4.cloned.1.call-start = ((), (), s32[]{:S(2)}) async-start(), calls=%async_computation.1 | async-start | bytes 1433600 | tf_op jit(solution)/shard_map/reduce_scatter | solution.py:21
  59.8 509.6 %all-gather.4.cloned.1.call-start = ((), (), s32[]{:S(2)}) async-start(), calls=%async_computation.2 | async-start | bytes 1433600 | tf_op jit(solution)/shard_map/all_gather | solution.py:27
  570.9 82.2 %copy-start.1 = (bf16[6,512]{1,0:T(8,128)(2,1)S(1)}, bf16[6,512]{1,0:T(8,128)(2,1)}, u32[]{:S(2)}) copy-start(bf16[6,512]{1,0:T(8,128)(2,1)} %param.9) | copy-start | bytes 18436
  647.6 54.5 %collective-permute-start = (bf16[8,512]{1,0:T(8,128)(2,1)S(1)}, bf16[8,512]{1,0:T(8,128)(2,1)S(1)}, u32[]{:S(2)}, u32[]{:S(2)}) collective-permute-start(bf16[8,512]{1,0:T(8,128)(2,1)S(1)} %convert.14), channel_id=1, source_target_pairs={{0,1},{1,2},{2,3},{3,4},{4,5},{5,6},{6,7},{7,8},{8,9},{9,10},{10,1... | collective-permute-start | bytes 24584
  650.4 54.7 %collective-permute-start.1 = (bf16[8,512]{1,0:T(8,128)(2,1)S(1)}, bf16[8,512]{1,0:T(8,128)(2,1)S(1)}, u32[]{:S(2)}, u32[]{:S(2)}) collective-permute-start(bf16[8,512]{1,0:T(8,128)(2,1)S(1)} %convert.14), channel_id=1, source_target_pairs={{0,2},{1,3},{2,4},{3,5},{4,6},{5,7},{6,8},{7,9},{8,10},{9,11},{10,... | collective-permute-start | bytes 24584
  651.8 49.0 %collective-permute-start.7 = (bf16[6,512]{1,0:T(8,128)(2,1)S(1)}, bf16[6,512]{1,0:T(8,128)(2,1)S(1)}, u32[]{:S(2)}, u32[]{:S(2)}) collective-permute-start(bf16[6,512]{1,0:T(8,128)(2,1)S(1)} %slice.10), channel_id=1, source_target_pairs={{0,8},{1,9},{2,10},{3,11},{4,12},{5,13},{6,14},{7,15},{8,16},{9,17... | collective-permute-start | bytes 18440
  698.2 13.3 %collective-permute-start.2 = (bf16[8,512]{1,0:T(8,128)(2,1)S(1)}, bf16[8,512]{1,0:T(8,128)(2,1)S(1)}, u32[]{:S(2)}, u32[]{:S(2)}) collective-permute-start(bf16[8,512]{1,0:T(8,128)(2,1)S(1)} %convert.14), channel_id=1, source_target_pairs={{0,3},{1,4},{2,5},{3,6},{4,7},{5,8},{6,9},{7,10},{8,11},{9,12},{10... | collective-permute-start | bytes 24584
  699.5 12.0 %collective-permute-start.3 = (bf16[8,512]{1,0:T(8,128)(2,1)S(1)}, bf16[8,512]{1,0:T(8,128)(2,1)S(1)}, u32[]{:S(2)}, u32[]{:S(2)}) collective-permute-start(bf16[8,512]{1,0:T(8,128)(2,1)S(1)} %convert.14), channel_id=1, source_target_pairs={{0,4},{1,5},{2,6},{3,7},{4,8},{5,9},{6,10},{7,11},{8,12},{9,13},{1... | collective-permute-start | bytes 24584
  700.8 10.7 %collective-permute-start.4 = (bf16[8,512]{1,0:T(8,128)(2,1)S(1)}, bf16[8,512]{1,0:T(8,128)(2,1)S(1)}, u32[]{:S(2)}, u32[]{:S(2)}) collective-permute-start(bf16[8,512]{1,0:T(8,128)(2,1)S(1)} %convert.14), channel_id=1, source_target_pairs={{0,5},{1,6},{2,7},{3,8},{4,9},{5,10},{6,11},{7,12},{8,13},{9,14},{... | collective-permute-start | bytes 24584
  702.1 9.3 %collective-permute-start.5 = (bf16[8,512]{1,0:T(8,128)(2,1)S(1)}, bf16[8,512]{1,0:T(8,128)(2,1)S(1)}, u32[]{:S(2)}, u32[]{:S(2)}) collective-permute-start(bf16[8,512]{1,0:T(8,128)(2,1)S(1)} %convert.14), channel_id=1, source_target_pairs={{0,6},{1,7},{2,8},{3,9},{4,10},{5,11},{6,12},{7,13},{8,14},{9,15},... | collective-permute-start | bytes 24584
  705.1 6.3 collective-permute-start.6
Sparse Core Ops, SparseCore 0:
  59.9 382.0 reduce-scatter.3
  445.7 123.6 all-gather.3
where the time goes:
time: 722 us; the launch traced here: 720 us
  waiting for transfers between devices  510 us (71%)
  blocking collectives  169 us (23%)
  starting transfers between devices  17.3 us (2%)
  between operations  14.9 us (2%)
    reduce_scatter x1, waiting for transfers between devices, body(): lax.psum_scatter(jnp.dot(segment, paired, preferred_element_type=jnp.floa...  382 us
    all_gather x1, waiting for transfers between devices, body(): summed_all = lax.all_gather(summed, 'dp', axis=0, tiled=True)  127 us
    unnamed x1, blocking collectives  76.3 us
    all_gather x1, blocking collectives, body(): lax.all_gather(tokens, 'tensor', axis=0, tiled=True)  49.4 us
    all_gather x1, blocking collectives, body(): lax.all_gather(out_grad, 'tensor', axis=0, tiled=True)  43.1 us
    unnamed x8, starting transfers between devices  17.2 us
  transfers between devices with their start and end apart: 10, of which 2 were waited for; matrix products, arithmetic and copies ran while one was open for 0% of the time, Pallas kernels for 0%

commit v1 on v0

v1 whole, which is shorter than its diff:
```python
import jax
import jax.numpy as jnp
from jax import lax
from jax.sharding import PartitionSpec as P


def gather_rows(block, axis):
    size = lax.axis_size(axis)
    copies = jnp.broadcast_to(block[None], (size, *block.shape))
    return lax.all_to_all(copies, axis, 0, 0, tiled=True)


def activate(summed, hidden_width):
    gate_values = summed[:, :hidden_width]
    up_values = summed[:, hidden_width:]
    return (jax.nn.silu(gate_values) * up_values).astype(jnp.bfloat16)


def body(tokens, gate_weight, up_weight, down_weight, out_grad):
    hidden_width = gate_weight.shape[1]
    own_rows, width = tokens.shape
    dp, tensor = lax.axis_size("dp"), lax.axis_size("tensor")
    rows = own_rows * tensor
    with jax.named_scope("gather_tokens"):
        both = gather_rows(jnp.stack([tokens, out_grad]), "tensor")
        gathered = both[:, 0].reshape(rows, width)
        cotangent = both[:, 1].reshape(rows, width)
    with jax.named_scope("gate_up_partial"):
        paired = jnp.concatenate([gate_weight, up_weight], axis=1)
        partial = jnp.dot(gathered, paired, preferred_element_type=jnp.float32)
    with jax.named_scope("gate_up_exchange"):
        parts = lax.all_to_all(partial.reshape(dp, rows // dp, -1), "dp", 0, 0, tiled=True)
    with jax.named_scope("activation"):
        hidden_share = activate(parts.sum(axis=0), hidden_width)
    with jax.named_scope("gather_hidden"):
        hidden = gather_rows(hidden_share, "dp").reshape(rows, hidden_width)
    with jax.named_scope("down"):
        mixed_partial = jnp.dot(hidden, down_weight, preferred_element_type=jnp.float32)
    with jax.named_scope("mixed_exchange"):
        mixed_parts = lax.all_to_all(
            mixed_partial.reshape(tensor, own_rows, width), "tensor", 0, 0, tiled=True
        )
        mixed = mixed_parts.sum(axis=0).astype(jnp.bfloat16)
    with jax.named_scope("down_grad"):
        contract = (((0,), (0,)), ((), ()))
        down_grad = lax.dot_general(hidden, cotangent, contract, preferred_element_type=jnp.float32)
    return (mixed, down_grad.astype(jnp.bfloat16))


def solution(mesh):
    placed = (
        P("tensor", "dp"),
        P("dp", "tensor"),
        P("dp", "tensor"),
        P("tensor", "dp"),
        P("tensor", "dp"),
    )
    return jax.shard_map(
        body,
        mesh=mesh,
        in_specs=placed,
        out_specs=(P("tensor", "dp"), P("tensor", "dp")),
        check_vma=False,
    )
```

time: 722 us -> 151 us (0.21)
  waiting for transfers between devices: 510 us -> 15.5 us
  blocking collectives: 169 us -> 119 us
  between operations: 14.9 us -> 0.75 us
  starting transfers between devices: 17.3 us -> 8.5 us
    reduce_scatter x1 -> x0, waiting for transfers between devices: 382 us -> none  [body(): lax.psum_scatter(jnp.dot(segment, paired, preferred_element_type=jnp.floa...]
    all_gather x1 -> x0, waiting for transfers between devices: 127 us -> none  [body(): summed_all = lax.all_gather(summed, 'dp', axis=0, tiled=True)]
    all_to_all x0 -> x3, blocking collectives: none -> 119 us  [the longest x1 64.8 us: body(): lax.all_to_all(partial.reshape(dp, rows // dp, -1), 'dp', 0, 0, tiled=True)]
    all_gather x2 -> x0, blocking collectives: 92.5 us -> none  [the longest x1 49.4 us: body(): lax.all_gather(tokens, 'tensor', axis=0, tiled=True)]
    unnamed x1 -> x0, blocking collectives: 76.3 us -> none
    unnamed x8 -> x0, starting transfers between devices: 17.2 us -> none
    all_to_all x0 -> x1, waiting for transfers between devices: none -> 15.5 us  [body(): lax.all_to_all(mixed_partial.reshape(tensor, own_rows, width), 'tensor',...]
    all_to_all x0 -> x1, starting transfers between devices: none -> 8.5 us  [body(): lax.all_to_all(mixed_partial.reshape(tensor, own_rows, width), 'tensor',...]
  transfers between devices with their start and end apart: 10 -> 1, of which waited for: 2 -> 1; matrix products, arithmetic and copies ran while one was open for 0% -> 1% of each run, Pallas kernels for 0% -> 0%
where the time goes in v1:
time: 151 us
  blocking collectives  119 us (79%)
  waiting for transfers between devices  15.5 us (10%)
  starting transfers between devices  8.5 us (6%)
  local copies, waits for them, and re-layouts  3.2 us (2%)
  matrix products  2.27 us (2%)
  other arithmetic  1.54 us (1%)
    all_to_all x1, blocking collectives, body(): lax.all_to_all(partial.reshape(dp, rows // dp, -1), 'dp', 0, 0, tiled=True)  64.8 us
    all_to_all x2, blocking collectives, gather_rows(): return lax.all_to_all(copies, axis, 0, 0, tiled=True)  54 us
    all_to_all x1, waiting for transfers between devices, body(): lax.all_to_all(mixed_partial.reshape(tensor, own_rows, width), 'tensor',...  15.5 us
    all_to_all x1, starting transfers between devices, body(): lax.all_to_all(mixed_partial.reshape(tensor, own_rows, width), 'tensor',...  8.5 us
  transfers between devices with their start and end apart: 1, of which 1 were waited for; matrix products, arithmetic and copies ran while one was open for 1% of the time, Pallas kernels for 0%

profile of v1, /device:TPU:1, one launch (start us, length us, event | category | flops | bytes accessed | tf_op | source)
XLA Modules:
  0.0 150.5 jit_solution(2907714136208225224)
XLA Ops:
  0.6 0.0 copy-start
  0.6 0.8 pad_maximum_fusion
  1.5 0.2 broadcast_in_dim.4
  1.7 0.0 copy-start.1
  1.7 0.0 copy-start.2
  1.7 27.4 %all_to_all.20 = bf16[32,2,6,512]{3,1,2,0:T(2,128)(2,1)S(1)} all-to-all(bf16[32,2,6,512]{3,1,2,0:T(2,128)(2,1)S(1)} %broadcast_in_dim.4), channel_id=1, replica_groups=mesh['dp'=24,'tensor'=32] {'tensor'}, dimensions={0} | all-to-all | bytes 786432 | tf_op jit(solution)/shard_map/gather_tokens/all_to_all | solution.py:10
  29.1 1.6 %slice_reduce_fusion = (bf16[32,6,512]{2,1,0:T(8,128)(2,1)S(1)}, bf16[32,6,512]{2,1,0:T(8,128)(2,1)S(1)}) fusion(bf16[32,2,6,512]{3,1,2,0:T(2,128)(2,1)S(1)} %all_to_all.20), kind=kLoop, calls=%fused_computation.7 | loop fusion | bytes 786432 | tf_op jit(solution)/shard_map/gather_tokens/slice | solution.py:27
  30.8 0.1 dot_general.13
  30.9 0.0 copy-done.1
  30.9 0.0 copy-done.2
  30.9 0.5 fusion
  31.4 64.8 %all_to_all.21 = f32[24,8,1792]{2,1,0:T(8,128)S(1)} all-to-all(f32[24,8,1792]{2,1,0:T(8,128)S(1)} %fusion), channel_id=1, replica_groups=mesh['dp'=24,'tensor'=32] {'dp'}, dimensions={0} | all-to-all | bytes 2752512 | tf_op jit(solution)/shard_map/gate_up_exchange/all_to_all | solution.py:32
  96.3 0.1 reduce_sum.18
  96.4 26.5 %all_to_all.22 = bf16[24,8,896]{2,1,0:T(8,128)(2,1)S(1)} all-to-all(bf16[24,8,896]{2,1,0:T(8,128)(2,1)S(1)} %broadcast_in_dim.5), channel_id=1, replica_groups=mesh['dp'=24,'tensor'=32] {'dp'}, dimensions={0} | all-to-all | bytes 688128 | tf_op jit(solution)/shard_map/gather_hidden/all_to_all | solution.py:10
  122.9 0.1 dot_general.15
  123.0 0.0 copy-done
  123.1 0.4 fusion.3
  123.4 1.0 copy.10
  124.5 8.5 %all-to-all-start.3 = ((f32[32,6,512]{2,1,0:T(8,128)}), f32[32,6,512]{2,1,0:T(8,128)S(1)}, u32[]{:S(2)}, u32[]{:S(2)}) async-start(f32[32,6,512]{2,1,0:T(8,128)} %copy.10), calls=%async_computation.3 | async-start | bytes 1048576 | tf_op jit(solution)/shard_map/mixed_exchange/all_to_all | solution.py:40
  133.0 0.1 squeeze.4
  133.1 1.4 convolution_convert_fusion
  134.4 15.5 %all-to-all-done.3 = f32[32,6,512]{2,1,0:T(8,128)S(1)} async-done(((f32[32,6,512]{2,1,0:T(8,128)}), f32[32,6,512]{2,1,0:T(8,128)S(1)}, u32[]{:S(2)}, u32[]{:S(2)}) %all-to-all-start.3) | async-done | bytes 393248 | tf_op jit(solution)/shard_map/mixed_exchange/all_to_all | solution.py:40
  149.9 0.7 reduce_sum.19
  (3 shorter events, 0.1 us)
Async XLA Ops:
  0.6 122.4 %copy-start = (bf16[896,512]{1,0:T(8,128)(2,1)S(1)}, bf16[896,512]{1,0:T(8,128)(2,1)}, u32[]{:S(2)}) copy-start(bf16[896,512]{1,0:T(8,128)(2,1)} %param.8) | copy-start | bytes 2752516
  1.7 29.2 %copy-start.1 = (bf16[512,896]{1,0:T(8,128)(2,1)S(1)}, bf16[512,896]{1,0:T(8,128)(2,1)}, u32[]{:S(2)}) copy-start(bf16[512,896]{1,0:T(8,128)(2,1)} %param.7) | copy-start | bytes 2752516
  1.7 29.2 %copy-start.2 = (bf16[512,896]{1,0:T(8,128)(2,1)S(1)}, bf16[512,896]{1,0:T(8,128)(2,1)}, u32[]{:S(2)}) copy-start(bf16[512,896]{1,0:T(8,128)(2,1)} %param.6) | copy-start | bytes 2752516
  124.5 25.4 %all-to-all-start.3 = ((f32[32,6,512]{2,1,0:T(8,128)}), f32[32,6,512]{2,1,0:T(8,128)S(1)}, u32[]{:S(2)}, u32[]{:S(2)}) async-start(f32[32,6,512]{2,1,0:T(8,128)} %copy.10), calls=%async_computation.3 | async-start | bytes 1048576 | tf_op jit(solution)/shard_map/mixed_exchange/all_to_all | solution.py:40

commit v2 on v1

v2 whole, which is shorter than its diff:
```python
import jax
import jax.numpy as jnp
from jax import lax
from jax.sharding import Mesh, PartitionSpec as P

Y_HI, CORES, X = 2, 2, 4
DP = ("y_hi", "z")
TENSOR = ("x", "y_lo", "core")
SWAP = [(0, 1), (1, 0)]


def gather(block, axes):
    copies = jnp.broadcast_to(block[None], (lax.axis_size(axes), *block.shape))
    return lax.all_to_all(copies, axes, 0, 0, tiled=True)


def body(tokens, gate_weight, up_weight, down_weight, out_grad):
    hidden_width = gate_weight.shape[1]
    own_rows, width = tokens.shape
    layers, tensor = lax.axis_size("z"), lax.axis_size(TENSOR)
    rows = own_rows * tensor
    with jax.named_scope("gather_tokens"):
        both = gather(jnp.concatenate([tokens, out_grad]), ("x", "y_lo"))
        first = lax.axis_index("core") == 0

        def pair(mine):
            other = lax.ppermute(mine, "core", SWAP)
            ordered = [jnp.where(first, mine, other), jnp.where(first, other, mine)]
            return jnp.stack(ordered, axis=1).reshape(rows, width)

        gathered = pair(both[:, :own_rows])
        cotangent = pair(both[:, own_rows:])
    with jax.named_scope("gate_up_partial"):
        paired = jnp.concatenate([gate_weight, up_weight], axis=1)
        partial = jnp.dot(gathered, paired, preferred_element_type=jnp.float32)
        partial = partial.astype(jnp.bfloat16).reshape(layers, rows // layers, 2 * hidden_width)
    with jax.named_scope("gate_up_exchange"):
        parts = lax.all_to_all(partial, "z", 0, 0, tiled=True)
        half = parts.astype(jnp.float32).sum(axis=0)
        summed = half + lax.ppermute(half, "y_hi", SWAP)
    with jax.named_scope("activation"):
        share = jax.nn.silu(summed[:, :hidden_width]) * summed[:, hidden_width:]
        share = share.astype(jnp.bfloat16)
    with jax.named_scope("gather_hidden"):
        hidden = gather(share, "z").reshape(rows, hidden_width)
    with jax.named_scope("down"):
        mixed_partial = jnp.dot(hidden, down_weight, preferred_element_type=jnp.float32)
    with jax.named_scope("mixed_exchange"):
        mixed_partial = mixed_partial.astype(jnp.bfloat16).reshape(tensor, own_rows, width)
        mixed_parts = lax.all_to_all(mixed_partial, TENSOR, 0, 0, tiled=True)
        mixed = mixed_parts.astype(jnp.float32).sum(axis=0).astype(jnp.bfloat16)
    with jax.named_scope("down_grad"):
        contract = (((0,), (0,)), ((), ()))
        down_grad = lax.dot_general(hidden, cotangent, contract, preferred_element_type=jnp.float32)
    return (mixed, down_grad.astype(jnp.bfloat16))


def solution(mesh):
    dp, tensor = mesh.shape["dp"], mesh.shape["tensor"]
    sizes = (Y_HI, dp // Y_HI, X, tensor // (X * CORES), CORES)
    fine = Mesh(mesh.devices.reshape(sizes), (*DP, *TENSOR))
    placed = (P(TENSOR, DP), P(DP, TENSOR), P(DP, TENSOR), P(TENSOR, DP), P(TENSOR, DP))
    return jax.shard_map(
        body,
        mesh=fine,
        in_specs=placed,
        out_specs=(P(TENSOR, DP), P(TENSOR, DP)),
        check_vma=False,
    )
```

time: 151 us -> 124 us (0.82)
  blocking collectives: 119 us -> 76.8 us
  starting transfers between devices: 8.5 us -> 23.4 us
  waiting for transfers between devices: 15.5 us -> 17.8 us
  local copies, waits for them, and re-layouts: 3.2 us -> 1.03 us
    all_to_all x3, blocking collectives: 119 us -> 76.8 us  [the longest x1 40.2 us: body(): parts = lax.all_to_all(partial, 'z', 0, 0, tiled=True)]
    ppermute x0 -> x3, starting transfers between devices: none -> 15.5 us  [the longest x2 10.8 us: pair(): other = lax.ppermute(mine, 'core', SWAP)]
    ppermute x0 -> x3, waiting for transfers between devices: none -> 7.93 us  [the longest x1 6.01 us: body(): summed = half + lax.ppermute(half, 'y_hi', SWAP)]
    all_to_all x1, waiting for transfers between devices: 15.5 us -> 9.88 us  [body(): mixed_parts = lax.all_to_all(mixed_partial, TENSOR, 0, 0, tiled=True)]
    slice x1, local copies, waits for them, and re-layouts: 1.65 us -> 0.04 us  [body(): cotangent = pair(both[:, own_rows:])]
  transfers between devices with their start and end apart: 1 -> 4, of which waited for: 1 -> 4; matrix products, arithmetic and copies ran while one was open for 1% -> 1% of each run, Pallas kernels for 0% -> 0%
where the time goes in v2:
time: 124 us
  blocking collectives  76.8 us (62%)
  starting transfers between devices  23.4 us (19%)
  waiting for transfers between devices  17.8 us (14%)
  matrix products  2.27 us (2%)
  other arithmetic  1.8 us (1%)
    all_to_all x1, blocking collectives, body(): parts = lax.all_to_all(partial, 'z', 0, 0, tiled=True)  40.2 us
    all_to_all x2, blocking collectives, gather(): return lax.all_to_all(copies, axes, 0, 0, tiled=True)  36.7 us
    ppermute x2, starting transfers between devices, pair(): other = lax.ppermute(mine, 'core', SWAP)  10.8 us
    all_to_all x1, waiting for transfers between devices, body(): mixed_parts = lax.all_to_all(mixed_partial, TENSOR, 0, 0, tiled=True)  9.88 us
    all_to_all x1, starting transfers between devices, body(): mixed_parts = lax.all_to_all(mixed_partial, TENSOR, 0, 0, tiled=True)  7.88 us
    ppermute x1, waiting for transfers between devices, body(): summed = half + lax.ppermute(half, 'y_hi', SWAP)  6.01 us
    ppermute x1, starting transfers between devices, body(): summed = half + lax.ppermute(half, 'y_hi', SWAP)  4.76 us
  transfers between devices with their start and end apart: 4, of which 4 were waited for; matrix products, arithmetic and copies ran while one was open for 1% of the time, Pallas kernels for 0%

profile of v2, /device:TPU:1, one launch (start us, length us, event | category | flops | bytes accessed | tf_op | source)
XLA Modules:
  0.0 124.0 jit_solution(5983890933043031577)
XLA Ops:
  0.6 0.0 copy-start
  0.6 0.8 pad_maximum_fusion.2
  1.5 15.8 %all_to_all.20 = bf16[16,12,512]{2,1,0:T(8,128)(2,1)S(1)} all-to-all(bf16[16,12,512]{2,1,0:T(8,128)(2,1)S(1)} %broadcast_in_dim.4), channel_id=1, replica_groups=mesh['y_hi'=2,'z'=12,'x'=4,'y_lo'=4,'core'=2] {'x','y_lo'}, dimensions={0} | all-to-all | bytes 393216 | tf_op jit(solution)/shard_map/gather_tokens/all_to_all | solution.py:14
  17.3 8.4 %collective-permute-start.2 = (bf16[16,6,512]{2,1,0:T(8,128)(2,1)S(1)}, bf16[16,6,512]{2,1,0:T(8,128)(2,1)S(1)}, u32[]{:S(2)}, u32[]{:S(2)}) collective-permute-start(bf16[16,6,512]{2,1,0:T(8,128)(2,1)S(1)} %slice.19), channel_id=1, source_target_pairs={{0,1},{1,0},{2,3},{3,2},{4,5},{5,4},{6,7},{7,6},{8,9},{9,8},{10,11... | collective-permute-start | bytes 294920 | tf_op jit(solution)/shard_map/gather_tokens/ppermute | solution.py:27
  25.7 1.0 collective-permute-done.2
  26.7 0.1 select_bitcast_fusion.1
  26.7 0.0 copy-start.1
  26.7 0.0 copy-start.2
  26.7 2.4 %collective-permute-start = (bf16[16,6,512]{2,1,0:T(8,128)(2,1)S(1)}, bf16[16,6,512]{2,1,0:T(8,128)(2,1)S(1)}, u32[]{:S(2)}, u32[]{:S(2)}) collective-permute-start(bf16[16,6,512]{2,1,0:T(8,128)(2,1)S(1)} %get-tuple-element.6), channel_id=1, source_target_pairs={{0,1},{1,0},{2,3},{3,2},{4,5},{5,4},{6,7},{7,6},{8,9},{9,8},{10,11... | collective-permute-start | bytes 294920 | tf_op jit(solution)/shard_map/gather_tokens/ppermute | solution.py:27
  29.1 1.0 collective-permute-done
  30.1 0.1 pad_maximum_fusion
  30.2 0.1 reshape.21
  30.3 0.0 copy-done.1
  30.3 0.0 copy-done.2
  30.3 0.5 convolution_convert_fusion
  30.9 40.2 %all_to_all.21 = bf16[12,16,1792]{2,1,0:T(8,128)(2,1)S(1)} all-to-all(bf16[12,16,1792]{2,1,0:T(8,128)(2,1)S(1)} %bitcast.19), channel_id=1, replica_groups=mesh['y_hi'=2,'z'=12,'x'=4,'y_lo'=4,'core'=2] {'z'}, dimensions={0} | all-to-all | bytes 1376256 | tf_op jit(solution)/shard_map/gate_up_exchange/all_to_all | solution.py:38
  71.0 0.1 convert_reduce_fusion
  71.1 4.8 %collective-permute-start.1 = (f32[16,1792]{1,0:T(8,128)S(1)}, f32[16,1792]{1,0:T(8,128)S(1)}, u32[]{:S(2)}, u32[]{:S(2)}) collective-permute-start(f32[16,1792]{1,0:T(8,128)S(1)} %convert_reduce_fusion), channel_id=1, source_target_pairs={{0,384},{384,0},{1,385},{385,1},{2,386},{386,2},{3,387},{387,3},{4... | collective-permute-start | bytes 344072 | tf_op jit(solution)/shard_map/gate_up_exchange/ppermute | solution.py:40
  75.9 6.0 %collective-permute-done.1 = f32[16,1792]{1,0:T(8,128)S(1)} collective-permute-done((f32[16,1792]{1,0:T(8,128)S(1)}, f32[16,1792]{1,0:T(8,128)S(1)}, u32[]{:S(2)}, u32[]{:S(2)}) %collective-permute-start.1) | collective-permute-done | bytes 114720 | tf_op jit(solution)/shard_map/gate_up_exchange/ppermute | solution.py:40
  82.0 20.9 %all_to_all.22 = bf16[12,16,896]{2,1,0:T(8,128)(2,1)S(1)} all-to-all(bf16[12,16,896]{2,1,0:T(8,128)(2,1)S(1)} %broadcast_in_dim.5), channel_id=1, replica_groups=mesh['y_hi'=2,'z'=12,'x'=4,'y_lo'=4,'core'=2] {'z'}, dimensions={0} | all-to-all | bytes 688128 | tf_op jit(solution)/shard_map/gather_hidden/all_to_all | solution.py:14
  102.9 0.0 copy-done
  102.9 0.4 convolution_convert_fusion.2
  103.3 0.8 reshape.24
  104.0 7.9 %all-to-all-start.3 = ((bf16[32,6,512]{2,1,0:T(8,128)(2,1)}), bf16[32,6,512]{2,1,0:T(8,128)(2,1)S(1)}, u32[]{:S(2)}, u32[]{:S(2)}) async-start(bf16[32,6,512]{2,1,0:T(8,128)(2,1)} %reshape.24), calls=%async_computation.3 | async-start | bytes 524288 | tf_op jit(solution)/shard_map/mixed_exchange/all_to_all | solution.py:50
  111.9 0.1 pad_maximum_fusion.1
  112.0 0.1 reshape.25
  112.1 1.4 %convolution_convert_fusion.1 = bf16[896,512]{1,0:T(8,128)(2,1)} fusion(bf16[192,896]{1,0:T(8,128)(2,1)S(1)} %bitcast.18, bf16[192,512]{1,0:T(8,128)(2,1)S(1)} %reshape.25), kind=kOutput, calls=%fused_computation.4 | convolution fusion | flops 176619520 | bytes 1458176 | tf_op jit(solution)/shard_map/down_grad/dot_general | solution.py:54
  113.4 9.9 %all-to-all-done.3 = bf16[32,6,512]{2,1,0:T(8,128)(2,1)S(1)} async-done(((bf16[32,6,512]{2,1,0:T(8,128)(2,1)}), bf16[32,6,512]{2,1,0:T(8,128)(2,1)S(1)}, u32[]{:S(2)}, u32[]{:S(2)}) %all-to-all-start.3) | async-done | bytes 196640 | tf_op jit(solution)/shard_map/mixed_exchange/all_to_all | solution.py:50
  123.3 0.7 reduce_sum.22
  (7 shorter events, 0.2 us)
Async XLA Ops:
  0.6 102.3 %copy-start = (bf16[896,512]{1,0:T(8,128)(2,1)S(1)}, bf16[896,512]{1,0:T(8,128)(2,1)}, u32[]{:S(2)}) copy-start(bf16[896,512]{1,0:T(8,128)(2,1)} %param.8) | copy-start | bytes 2752516
  17.3 9.4 %collective-permute-start.2 = (bf16[16,6,512]{2,1,0:T(8,128)(2,1)S(1)}, bf16[16,6,512]{2,1,0:T(8,128)(2,1)S(1)}, u32[]{:S(2)}, u32[]{:S(2)}) collective-permute-start(bf16[16,6,512]{2,1,0:T(8,128)(2,1)S(1)} %slice.19), channel_id=1, source_target_pairs={{0,1},{1,0},{2,3},{3,2},{4,5},{5,4},{6,7},{7,6},{8,9},{9,8},{10,11... | collective-permute-start | bytes 294920 | tf_op jit(solution)/shard_map/gather_tokens/ppermute | solution.py:27
  26.7 3.6 %copy-start.1 = (bf16[512,896]{1,0:T(8,128)(2,1)S(1)}, bf16[512,896]{1,0:T(8,128)(2,1)}, u32[]{:S(2)}) copy-start(bf16[512,896]{1,0:T(8,128)(2,1)} %param.7) | copy-start | bytes 2752516
  26.7 3.6 %copy-start.2 = (bf16[512,896]{1,0:T(8,128)(2,1)S(1)}, bf16[512,896]{1,0:T(8,128)(2,1)}, u32[]{:S(2)}) copy-start(bf16[512,896]{1,0:T(8,128)(2,1)} %param.6) | copy-start | bytes 2752516
  26.7 3.4 %collective-permute-start = (bf16[16,6,512]{2,1,0:T(8,128)(2,1)S(1)}, bf16[16,6,512]{2,1,0:T(8,128)(2,1)S(1)}, u32[]{:S(2)}, u32[]{:S(2)}) collective-permute-start(bf16[16,6,512]{2,1,0:T(8,128)(2,1)S(1)} %get-tuple-element.6), channel_id=1, source_target_pairs={{0,1},{1,0},{2,3},{3,2},{4,5},{5,4},{6,7},{7,6},{8,9},{9,8},{10,11... | collective-permute-start | bytes 294920 | tf_op jit(solution)/shard_map/gather_tokens/ppermute | solution.py:27
  71.1 10.8 %collective-permute-start.1 = (f32[16,1792]{1,0:T(8,128)S(1)}, f32[16,1792]{1,0:T(8,128)S(1)}, u32[]{:S(2)}, u32[]{:S(2)}) collective-permute-start(f32[16,1792]{1,0:T(8,128)S(1)} %convert_reduce_fusion), channel_id=1, source_target_pairs={{0,384},{384,0},{1,385},{385,1},{2,386},{386,2},{3,387},{387,3},{4... | collective-permute-start | bytes 344072 | tf_op jit(solution)/shard_map/gate_up_exchange/ppermute | solution.py:40
  104.0 19.3 %all-to-all-start.3 = ((bf16[32,6,512]{2,1,0:T(8,128)(2,1)}), bf16[32,6,512]{2,1,0:T(8,128)(2,1)S(1)}, u32[]{:S(2)}, u32[]{:S(2)}) async-start(bf16[32,6,512]{2,1,0:T(8,128)(2,1)} %reshape.24), calls=%async_computation.3 | async-start | bytes 524288 | tf_op jit(solution)/shard_map/mixed_exchange/all_to_all | solution.py:50

commit v3 on v2

--- a/solution.py
+++ b/solution.py
@@ -17,19 +17,13 @@
 def body(tokens, gate_weight, up_weight, down_weight, out_grad):
     hidden_width = gate_weight.shape[1]
     own_rows, width = tokens.shape
-    layers, tensor = lax.axis_size("z"), lax.axis_size(TENSOR)
-    rows = own_rows * tensor
+    layers, chips = lax.axis_size("z"), lax.axis_size(("x", "y_lo"))
+    rows = own_rows * chips * CORES
     with jax.named_scope("gather_tokens"):
-        both = gather(jnp.concatenate([tokens, out_grad]), ("x", "y_lo"))
-        first = lax.axis_index("core") == 0
-
-        def pair(mine):
-            other = lax.ppermute(mine, "core", SWAP)
-            ordered = [jnp.where(first, mine, other), jnp.where(first, other, mine)]
-            return jnp.stack(ordered, axis=1).reshape(rows, width)
-
-        gathered = pair(both[:, :own_rows])
-        cotangent = pair(both[:, own_rows:])
+        mine = gather(jnp.concatenate([tokens, out_grad]), ("x", "y_lo"))
+        both = jnp.stack([mine, lax.ppermute(mine, "core", SWAP)])
+        gathered = both[:, :, :own_rows].reshape(rows, width)
+        cotangent = both[:, :, own_rows:].reshape(rows, width)
     with jax.named_scope("gate_up_partial"):
         paired = jnp.concatenate([gate_weight, up_weight], axis=1)
         partial = jnp.dot(gathered, paired, preferred_element_type=jnp.float32)
@@ -46,8 +40,10 @@
     with jax.named_scope("down"):
         mixed_partial = jnp.dot(hidden, down_weight, preferred_element_type=jnp.float32)
     with jax.named_scope("mixed_exchange"):
-        mixed_partial = mixed_partial.astype(jnp.bfloat16).reshape(tensor, own_rows, width)
-        mixed_parts = lax.all_to_all(mixed_partial, TENSOR, 0, 0, tiled=True)
+        kept, sent = mixed_partial[: rows // CORES], mixed_partial[rows // CORES :]
+        chip_sum = kept + lax.ppermute(sent, "core", SWAP)
+        chip_sum = chip_sum.astype(jnp.bfloat16).reshape(chips, own_rows, width)
+        mixed_parts = lax.all_to_all(chip_sum, ("x", "y_lo"), 0, 0, tiled=True)
         mixed = mixed_parts.astype(jnp.float32).sum(axis=0).astype(jnp.bfloat16)
     with jax.named_scope("down_grad"):
         contract = (((0,), (0,)), ((), ()))

time: 124 us -> 120 us (0.968)
  waiting for transfers between devices: 17.8 us -> 14 us
    all_to_all x1, starting transfers between devices: 7.88 us -> 3.51 us  [body(): mixed_parts = lax.all_to_all(chip_sum, ('x', 'y_lo'), 0, 0, tiled=True)]
    all_to_all x1, waiting for transfers between devices: 9.88 us -> 5.84 us  [body(): mixed_parts = lax.all_to_all(chip_sum, ('x', 'y_lo'), 0, 0, tiled=True)]
    ppermute x2, starting transfers between devices: 10.8 us -> 14.6 us  [the longest x1 8.37 us: body(): both = jnp.stack([mine, lax.ppermute(mine, 'core', SWAP)])]
where the time goes in v3:
time: 120 us; the launch traced here: 119 us
  blocking collectives  77 us (64%)
  starting transfers between devices  22.9 us (19%)
  waiting for transfers between devices  14 us (12%)
  matrix products  2.27 us (2%)
  other arithmetic  1.72 us (1%)
    all_to_all x1, blocking collectives, body(): parts = lax.all_to_all(partial, 'z', 0, 0, tiled=True)  40.2 us
    all_to_all x2, blocking collectives, gather(): return lax.all_to_all(copies, axes, 0, 0, tiled=True)  36.8 us
    ppermute x1, starting transfers between devices, body(): both = jnp.stack([mine, lax.ppermute(mine, 'core', SWAP)])  8.37 us
    ppermute x1, starting transfers between devices, body(): chip_sum = kept + lax.ppermute(sent, 'core', SWAP)  6.26 us
    ppermute x1, waiting for transfers between devices, body(): summed = half + lax.ppermute(half, 'y_hi', SWAP)  6.03 us
    all_to_all x1, waiting for transfers between devices, body(): mixed_parts = lax.all_to_all(chip_sum, ('x', 'y_lo'), 0, 0, tiled=True)  5.84 us
    ppermute x1, starting transfers between devices, body(): summed = half + lax.ppermute(half, 'y_hi', SWAP)  4.74 us
    all_to_all x1, starting transfers between devices, body(): mixed_parts = lax.all_to_all(chip_sum, ('x', 'y_lo'), 0, 0, tiled=True)  3.51 us
  transfers between devices with their start and end apart: 4, of which 4 were waited for; matrix products, arithmetic and copies ran while one was open for 1% of the time, Pallas kernels for 0%

profile of v3, /device:TPU:1, one launch (start us, length us, event | category | flops | bytes accessed | tf_op | source)
XLA Modules:
  0.0 119.5 jit_solution(12745554460966790120)
XLA Ops:
  0.6 0.0 copy-start
  0.6 0.8 pad_maximum_fusion.1
  1.5 0.0 copy-start.1
  1.5 0.0 copy-start.2
  1.5 15.9 %all_to_all.20 = bf16[16,12,512]{2,1,0:T(8,128)(2,1)S(1)} all-to-all(bf16[16,12,512]{2,1,0:T(8,128)(2,1)S(1)} %broadcast_in_dim.4), channel_id=1, replica_groups=mesh['y_hi'=2,'z'=12,'x'=4,'y_lo'=4,'core'=2] {'x','y_lo'}, dimensions={0} | all-to-all | bytes 393216 | tf_op jit(solution)/shard_map/gather_tokens/all_to_all | solution.py:14
  17.4 8.4 %collective-permute-start = (bf16[16,12,512]{2,1,0:T(8,128)(2,1)S(1)}, bf16[16,12,512]{2,1,0:T(8,128)(2,1)S(1)}, u32[]{:S(2)}, u32[]{:S(2)}) collective-permute-start(bf16[16,12,512]{2,1,0:T(8,128)(2,1)S(1)} %all_to_all.20), channel_id=1, source_target_pairs={{0,1},{1,0},{2,3},{3,2},{4,5},{5,4},{6,7},{7,6},{8,9},{9,8},{10,11... | collective-permute-start | bytes 589832 | tf_op jit(solution)/shard_map/gather_tokens/ppermute | solution.py:24
  25.8 1.1 collective-permute-done
  26.9 0.1 pad_maximum_fusion
  27.0 0.1 reshape.21
  27.1 0.0 copy-done.1
  27.1 0.0 copy-done.2
  27.1 0.5 convolution_convert_fusion
  27.7 40.2 %all_to_all.21 = bf16[12,16,1792]{2,1,0:T(8,128)(2,1)S(1)} all-to-all(bf16[12,16,1792]{2,1,0:T(8,128)(2,1)S(1)} %bitcast.12), channel_id=1, replica_groups=mesh['y_hi'=2,'z'=12,'x'=4,'y_lo'=4,'core'=2] {'z'}, dimensions={0} | all-to-all | bytes 1376256 | tf_op jit(solution)/shard_map/gate_up_exchange/all_to_all | solution.py:32
  67.9 0.1 convert_reduce_fusion
  68.0 4.7 %collective-permute-start.1 = (f32[16,1792]{1,0:T(8,128)S(1)}, f32[16,1792]{1,0:T(8,128)S(1)}, u32[]{:S(2)}, u32[]{:S(2)}) collective-permute-start(f32[16,1792]{1,0:T(8,128)S(1)} %convert_reduce_fusion), channel_id=1, source_target_pairs={{0,384},{384,0},{1,385},{385,1},{2,386},{386,2},{3,387},{387,3},{4... | collective-permute-start | bytes 344072 | tf_op jit(solution)/shard_map/gate_up_exchange/ppermute | solution.py:34
  72.7 6.0 %collective-permute-done.1 = f32[16,1792]{1,0:T(8,128)S(1)} collective-permute-done((f32[16,1792]{1,0:T(8,128)S(1)}, f32[16,1792]{1,0:T(8,128)S(1)}, u32[]{:S(2)}, u32[]{:S(2)}) %collective-permute-start.1) | collective-permute-done | bytes 114720 | tf_op jit(solution)/shard_map/gate_up_exchange/ppermute | solution.py:34
  78.8 20.9 %all_to_all.22 = bf16[12,16,896]{2,1,0:T(8,128)(2,1)S(1)} all-to-all(bf16[12,16,896]{2,1,0:T(8,128)(2,1)S(1)} %broadcast_in_dim.5), channel_id=1, replica_groups=mesh['y_hi'=2,'z'=12,'x'=4,'y_lo'=4,'core'=2] {'z'}, dimensions={0} | all-to-all | bytes 688128 | tf_op jit(solution)/shard_map/gather_hidden/all_to_all | solution.py:14
  99.7 0.0 copy-done
  99.7 0.4 fusion.7
  100.1 6.3 %collective-permute-start.2 = (f32[96,512]{1,0:T(8,128)S(1)}, f32[96,512]{1,0:T(8,128)S(1)}, u32[]{:S(2)}, u32[]{:S(2)}) collective-permute-start(f32[96,512]{1,0:T(8,128)S(1)} %slice.29), channel_id=1, source_target_pairs={{0,1},{1,0},{2,3},{3,2},{4,5},{5,4},{6,7},{7,6},{8,9},{9,8},{10,11... | collective-permute-start | bytes 589832 | tf_op jit(solution)/shard_map/mixed_exchange/ppermute | solution.py:44
  106.4 0.1 reshape.25
  106.4 1.0 collective-permute-done.2
  107.5 0.7 reshape.24
  108.1 3.5 %all-to-all-start.3 = ((bf16[16,6,512]{2,1,0:T(8,128)(2,1)}), bf16[16,6,512]{2,1,0:T(8,128)(2,1)S(1)}, u32[]{:S(2)}, u32[]{:S(2)}) async-start(bf16[16,6,512]{2,1,0:T(8,128)(2,1)} %reshape.24), calls=%async_computation.3 | async-start | bytes 262144 | tf_op jit(solution)/shard_map/mixed_exchange/all_to_all | solution.py:46
  111.6 1.4 %convolution_convert_fusion.1 = bf16[896,512]{1,0:T(8,128)(2,1)} fusion(bf16[192,896]{1,0:T(8,128)(2,1)S(1)} %bitcast.10, bf16[192,512]{1,0:T(8,128)(2,1)S(1)} %reshape.25), kind=kOutput, calls=%fused_computation.4 | convolution fusion | flops 176619520 | bytes 1458176 | tf_op jit(solution)/shard_map/down_grad/dot_general | solution.py:50
  113.0 5.8 %all-to-all-done.3 = bf16[16,6,512]{2,1,0:T(8,128)(2,1)S(1)} async-done(((bf16[16,6,512]{2,1,0:T(8,128)(2,1)}), bf16[16,6,512]{2,1,0:T(8,128)(2,1)S(1)}, u32[]{:S(2)}, u32[]{:S(2)}) %all-to-all-start.3) | async-done | bytes 98336 | tf_op jit(solution)/shard_map/mixed_exchange/all_to_all | solution.py:46
  118.9 0.6 reduce_sum.22
  (6 shorter events, 0.1 us)
Async XLA Ops:
  0.6 99.1 %copy-start = (bf16[896,512]{1,0:T(8,128)(2,1)S(1)}, bf16[896,512]{1,0:T(8,128)(2,1)}, u32[]{:S(2)}) copy-start(bf16[896,512]{1,0:T(8,128)(2,1)} %param.8) | copy-start | bytes 2752516
  1.5 25.6 %copy-start.1 = (bf16[512,896]{1,0:T(8,128)(2,1)S(1)}, bf16[512,896]{1,0:T(8,128)(2,1)}, u32[]{:S(2)}) copy-start(bf16[512,896]{1,0:T(8,128)(2,1)} %param.7) | copy-start | bytes 2752516
  1.5 25.6 %copy-start.2 = (bf16[512,896]{1,0:T(8,128)(2,1)S(1)}, bf16[512,896]{1,0:T(8,128)(2,1)}, u32[]{:S(2)}) copy-start(bf16[512,896]{1,0:T(8,128)(2,1)} %param.6) | copy-start | bytes 2752516
  17.4 9.5 %collective-permute-start = (bf16[16,12,512]{2,1,0:T(8,128)(2,1)S(1)}, bf16[16,12,512]{2,1,0:T(8,128)(2,1)S(1)}, u32[]{:S(2)}, u32[]{:S(2)}) collective-permute-start(bf16[16,12,512]{2,1,0:T(8,128)(2,1)S(1)} %all_to_all.20), channel_id=1, source_target_pairs={{0,1},{1,0},{2,3},{3,2},{4,5},{5,4},{6,7},{7,6},{8,9},{9,8},{10,11... | collective-permute-start | bytes 589832 | tf_op jit(solution)/shard_map/gather_tokens/ppermute | solution.py:24
  68.0 10.8 %collective-permute-start.1 = (f32[16,1792]{1,0:T(8,128)S(1)}, f32[16,1792]{1,0:T(8,128)S(1)}, u32[]{:S(2)}, u32[]{:S(2)}) collective-permute-start(f32[16,1792]{1,0:T(8,128)S(1)} %convert_reduce_fusion), channel_id=1, source_target_pairs={{0,384},{384,0},{1,385},{385,1},{2,386},{386,2},{3,387},{387,3},{4... | collective-permute-start | bytes 344072 | tf_op jit(solution)/shard_map/gate_up_exchange/ppermute | solution.py:34
  100.1 7.3 %collective-permute-start.2 = (f32[96,512]{1,0:T(8,128)S(1)}, f32[96,512]{1,0:T(8,128)S(1)}, u32[]{:S(2)}, u32[]{:S(2)}) collective-permute-start(f32[96,512]{1,0:T(8,128)S(1)} %slice.29), channel_id=1, source_target_pairs={{0,1},{1,0},{2,3},{3,2},{4,5},{5,4},{6,7},{7,6},{8,9},{9,8},{10,11... | collective-permute-start | bytes 589832 | tf_op jit(solution)/shard_map/mixed_exchange/ppermute | solution.py:44
  108.1 10.7 %all-to-all-start.3 = ((bf16[16,6,512]{2,1,0:T(8,128)(2,1)}), bf16[16,6,512]{2,1,0:T(8,128)(2,1)S(1)}, u32[]{:S(2)}, u32[]{:S(2)}) async-start(bf16[16,6,512]{2,1,0:T(8,128)(2,1)} %reshape.24), calls=%async_computation.3 | async-start | bytes 262144 | tf_op jit(solution)/shard_map/mixed_exchange/all_to_all | solution.py:46

commit v4 on v3

--- a/solution.py
+++ b/solution.py
@@ -31,7 +31,7 @@
     with jax.named_scope("gate_up_exchange"):
         parts = lax.all_to_all(partial, "z", 0, 0, tiled=True)
         half = parts.astype(jnp.float32).sum(axis=0)
-        summed = half + lax.ppermute(half, "y_hi", SWAP)
+        summed = lax.all_gather(half, "y_hi").sum(axis=0)
     with jax.named_scope("activation"):
         share = jax.nn.silu(summed[:, :hidden_width]) * summed[:, hidden_width:]
         share = share.astype(jnp.bfloat16)
@@ -41,7 +41,9 @@
         mixed_partial = jnp.dot(hidden, down_weight, preferred_element_type=jnp.float32)
     with jax.named_scope("mixed_exchange"):
         kept, sent = mixed_partial[: rows // CORES], mixed_partial[rows // CORES :]
-        chip_sum = kept + lax.ppermute(sent, "core", SWAP)
+        chip_sum = kept + lax.dynamic_index_in_dim(
+            lax.all_gather(sent, "core"), 1 - lax.axis_index("core"), 0, keepdims=False
+        )
         chip_sum = chip_sum.astype(jnp.bfloat16).reshape(chips, own_rows, width)
         mixed_parts = lax.all_to_all(chip_sum, ("x", "y_lo"), 0, 0, tiled=True)
         mixed = mixed_parts.astype(jnp.float32).sum(axis=0).astype(jnp.bfloat16)

time: 120 us -> 118 us (0.983)
  waiting for transfers between devices: 14 us -> 22.8 us
  blocking collectives: 77 us -> 70.9 us
  starting transfers between devices: 22.9 us -> 17.9 us
    all_to_all x2 -> x1, blocking collectives: 36.8 us -> 15.9 us  [gather(): return lax.all_to_all(copies, axes, 0, 0, tiled=True)]
    all_to_all x0 -> x1, waiting for transfers between devices: none -> 15.8 us  [gather(): return lax.all_to_all(copies, axes, 0, 0, tiled=True)]
    all_gather x0 -> x2, blocking collectives: none -> 14.8 us  [the longest x1 9.56 us: body(): summed = lax.all_gather(half, 'y_hi').sum(axis=0)]
    ppermute x2 -> x0, starting transfers between devices: 11 us -> none  [the longest x1 6.26 us: body(): chip_sum = kept + lax.ppermute(sent, 'core', SWAP)]
    ppermute x2 -> x0, waiting for transfers between devices: 7 us -> none  [the longest x1 6.03 us: body(): summed = half + lax.ppermute(half, 'y_hi', SWAP)]
    all_to_all x0 -> x1, starting transfers between devices: none -> 6.01 us  [gather(): return lax.all_to_all(copies, axes, 0, 0, tiled=True)]
  transfers between devices with their start and end apart: 4 -> 3, of which waited for: 4 -> 3; matrix products, arithmetic and copies ran while one was open for 1% -> 1% of each run, Pallas kernels for 0% -> 0%
where the time goes in v4:
time: 118 us
  blocking collectives  70.9 us (60%)
  waiting for transfers between devices  22.8 us (19%)
  starting transfers between devices  17.9 us (15%)
  matrix products  2.27 us (2%)
  other arithmetic  1.72 us (1%)
  local copies, waits for them, and re-layouts  1.64 us (1%)
    all_to_all x1, blocking collectives, body(): parts = lax.all_to_all(partial, 'z', 0, 0, tiled=True)  40.2 us
    all_to_all x1, blocking collectives, gather(): return lax.all_to_all(copies, axes, 0, 0, tiled=True)  15.9 us
    all_to_all x1, waiting for transfers between devices, gather(): return lax.all_to_all(copies, axes, 0, 0, tiled=True)  15.8 us
    all_gather x1, blocking collectives, body(): summed = lax.all_gather(half, 'y_hi').sum(axis=0)  9.56 us
    ppermute x1, starting transfers between devices, body(): both = jnp.stack([mine, lax.ppermute(mine, 'core', SWAP)])  8.37 us
    all_to_all x1, starting transfers between devices, gather(): return lax.all_to_all(copies, axes, 0, 0, tiled=True)  6.01 us
    all_to_all x1, waiting for transfers between devices, body(): mixed_parts = lax.all_to_all(chip_sum, ('x', 'y_lo'), 0, 0, tiled=True)  5.84 us
    all_gather x1, blocking collectives, body(): lax.all_gather(sent, 'core')  5.24 us
  transfers between devices with their start and end apart: 3, of which 3 were waited for; matrix products, arithmetic and copies ran while one was open for 1% of the time, Pallas kernels for 0%

profile of v4, /device:TPU:1, one launch (start us, length us, event | category | flops | bytes accessed | tf_op | source)
XLA Modules:
  0.0 118.0 jit_solution(10161508372626990009)
XLA Ops:
  0.6 0.0 copy-start
  0.6 0.8 pad_maximum_fusion.1
  1.5 0.0 copy-start.1
  1.5 0.0 copy-start.2
  1.5 15.9 %all_to_all.20 = bf16[16,12,512]{2,1,0:T(8,128)(2,1)S(1)} all-to-all(bf16[16,12,512]{2,1,0:T(8,128)(2,1)S(1)} %broadcast_in_dim.4), channel_id=1, replica_groups=mesh['y_hi'=2,'z'=12,'x'=4,'y_lo'=4,'core'=2] {'x','y_lo'}, dimensions={0} | all-to-all | bytes 393216 | tf_op jit(solution)/shard_map/gather_tokens/all_to_all | solution.py:14
  17.4 8.4 %collective-permute-start = (bf16[16,12,512]{2,1,0:T(8,128)(2,1)S(1)}, bf16[16,12,512]{2,1,0:T(8,128)(2,1)S(1)}, u32[]{:S(2)}, u32[]{:S(2)}) collective-permute-start(bf16[16,12,512]{2,1,0:T(8,128)(2,1)S(1)} %all_to_all.20), channel_id=1, source_target_pairs={{0,1},{1,0},{2,3},{3,2},{4,5},{5,4},{6,7},{7,6},{8,9},{9,8},{10,11... | collective-permute-start | bytes 589832 | tf_op jit(solution)/shard_map/gather_tokens/ppermute | solution.py:24
  25.8 1.1 collective-permute-done
  26.9 0.1 pad_maximum_fusion
  27.0 0.1 reshape.21
  27.1 0.0 copy-done.1
  27.1 0.0 copy-done.2
  27.1 0.5 convolution_convert_fusion
  27.7 40.2 %all_to_all.21 = bf16[12,16,1792]{2,1,0:T(8,128)(2,1)S(1)} all-to-all(bf16[12,16,1792]{2,1,0:T(8,128)(2,1)S(1)} %bitcast.18), channel_id=1, replica_groups=mesh['y_hi'=2,'z'=12,'x'=4,'y_lo'=4,'core'=2] {'z'}, dimensions={0} | all-to-all | bytes 1376256 | tf_op jit(solution)/shard_map/gate_up_exchange/all_to_all | solution.py:32
  67.9 0.1 convert_reduce_fusion
  68.0 9.6 %all-gather = f32[32,1792]{1,0:T(8,128)S(1)} all-gather(f32[16,1792]{1,0:T(8,128)S(1)} %convert_reduce_fusion), channel_id=2, replica_groups=mesh['y_hi'=2,'z'=12,'x'=4,'y_lo'=4,'core'=2] {'y_hi'}, dimensions={0}, use_global_device_ids=true | all-gather | bytes 344064 | tf_op jit(solution)/shard_map/gate_up_exchange/all_gather | solution.py:34
  77.6 0.8 broadcast_in_dim.5
  78.3 6.0 %all-to-all-start.2 = ((bf16[12,16,896]{2,1,0:T(8,128)(2,1)}), bf16[12,16,896]{2,1,0:T(8,128)(2,1)S(1)}, u32[]{:S(2)}, u32[]{:S(2)}) async-start(bf16[12,16,896]{2,1,0:T(8,128)(2,1)} %broadcast_in_dim.5), calls=%async_computation.2 | async-start | bytes 688128 | tf_op jit(solution)/shard_map/gather_hidden/all_to_all | solution.py:14
  84.4 0.1 reshape.25
  84.4 15.8 %all-to-all-done.2 = bf16[12,16,896]{2,1,0:T(8,128)(2,1)S(1)} async-done(((bf16[12,16,896]{2,1,0:T(8,128)(2,1)}), bf16[12,16,896]{2,1,0:T(8,128)(2,1)S(1)}, u32[]{:S(2)}, u32[]{:S(2)}) %all-to-all-start.2) | async-done | bytes 344096 | tf_op jit(solution)/shard_map/gather_hidden/all_to_all | solution.py:14
  100.2 0.0 copy-done
  100.2 0.4 fusion.7
  100.6 5.2 %all-gather.1 = f32[192,512]{1,0:T(8,128)S(1)} all-gather(f32[96,512]{1,0:T(8,128)S(1)} %slice.29), channel_id=3, replica_groups=mesh['y_hi'=2,'z'=12,'x'=4,'y_lo'=4,'core'=2] {'core'}, dimensions={0}, use_global_device_ids=true | all-gather | bytes 589824 | tf_op jit(solution)/shard_map/mixed_exchange/all_gather | solution.py:45
  105.9 0.7 reshape.24
  106.6 3.5 %all-to-all-start.3 = ((bf16[16,6,512]{2,1,0:T(8,128)(2,1)}), bf16[16,6,512]{2,1,0:T(8,128)(2,1)S(1)}, u32[]{:S(2)}, u32[]{:S(2)}) async-start(bf16[16,6,512]{2,1,0:T(8,128)(2,1)} %reshape.24), calls=%async_computation.3 | async-start | bytes 262144 | tf_op jit(solution)/shard_map/mixed_exchange/all_to_all | solution.py:48
  110.1 1.4 %convolution_convert_fusion.1 = bf16[896,512]{1,0:T(8,128)(2,1)} fusion(bf16[192,896]{1,0:T(8,128)(2,1)S(1)} %bitcast.14, bf16[192,512]{1,0:T(8,128)(2,1)S(1)} %reshape.25), kind=kOutput, calls=%fused_computation.4 | convolution fusion | flops 176619520 | bytes 1458176 | tf_op jit(solution)/shard_map/down_grad/dot_general | solution.py:52
  111.5 5.8 %all-to-all-done.3 = bf16[16,6,512]{2,1,0:T(8,128)(2,1)S(1)} async-done(((bf16[16,6,512]{2,1,0:T(8,128)(2,1)}), bf16[16,6,512]{2,1,0:T(8,128)(2,1)S(1)}, u32[]{:S(2)}, u32[]{:S(2)}) %all-to-all-start.3) | async-done | bytes 98336 | tf_op jit(solution)/shard_map/mixed_exchange/all_to_all | solution.py:48
  117.3 0.6 reduce_sum.32
  (5 shorter events, 0.1 us)
Async XLA Ops:
  0.6 99.6 %copy-start = (bf16[896,512]{1,0:T(8,128)(2,1)S(1)}, bf16[896,512]{1,0:T(8,128)(2,1)}, u32[]{:S(2)}) copy-start(bf16[896,512]{1,0:T(8,128)(2,1)} %param.8) | copy-start | bytes 2752516
  1.5 25.6 %copy-start.1 = (bf16[512,896]{1,0:T(8,128)(2,1)S(1)}, bf16[512,896]{1,0:T(8,128)(2,1)}, u32[]{:S(2)}) copy-start(bf16[512,896]{1,0:T(8,128)(2,1)} %param.7) | copy-start | bytes 2752516
  1.5 25.6 %copy-start.2 = (bf16[512,896]{1,0:T(8,128)(2,1)S(1)}, bf16[512,896]{1,0:T(8,128)(2,1)}, u32[]{:S(2)}) copy-start(bf16[512,896]{1,0:T(8,128)(2,1)} %param.6) | copy-start | bytes 2752516
  17.4 9.5 %collective-permute-start = (bf16[16,12,512]{2,1,0:T(8,128)(2,1)S(1)}, bf16[16,12,512]{2,1,0:T(8,128)(2,1)S(1)}, u32[]{:S(2)}, u32[]{:S(2)}) collective-permute-start(bf16[16,12,512]{2,1,0:T(8,128)(2,1)S(1)} %all_to_all.20), channel_id=1, source_target_pairs={{0,1},{1,0},{2,3},{3,2},{4,5},{5,4},{6,7},{7,6},{8,9},{9,8},{10,11... | collective-permute-start | bytes 589832 | tf_op jit(solution)/shard_map/gather_tokens/ppermute | solution.py:24
  78.3 21.9 %all-to-all-start.2 = ((bf16[12,16,896]{2,1,0:T(8,128)(2,1)}), bf16[12,16,896]{2,1,0:T(8,128)(2,1)S(1)}, u32[]{:S(2)}, u32[]{:S(2)}) async-start(bf16[12,16,896]{2,1,0:T(8,128)(2,1)} %broadcast_in_dim.5), calls=%async_computation.2 | async-start | bytes 688128 | tf_op jit(solution)/shard_map/gather_hidden/all_to_all | solution.py:14
  106.6 10.7 %all-to-all-start.3 = ((bf16[16,6,512]{2,1,0:T(8,128)(2,1)}), bf16[16,6,512]{2,1,0:T(8,128)(2,1)S(1)}, u32[]{:S(2)}, u32[]{:S(2)}) async-start(bf16[16,6,512]{2,1,0:T(8,128)(2,1)} %reshape.24), calls=%async_computation.3 | async-start | bytes 262144 | tf_op jit(solution)/shard_map/mixed_exchange/all_to_all | solution.py:48
